TPU v7x, 32 devices: a whole 2x2x4 slice. The times are simulated.
32 devices in a mesh: alpha: 4 (over y, x), beta: 8 (over z, core).
Axes of the slice: x: 2, y: 2, z: 4, core: 2. Of those that a mesh axis runs over, the one named last changes fastest.
Arguments:
- coefficients: bfloat16 [1024, 2048], P('alpha', 'beta'), may hold values from -6 to 6
- diagonal: float32 [1024, 2048], P('alpha', 'beta'), may hold values from 0.3 to 3
- integrals: bfloat16 [324, 324], replicated, may hold values from -0.02734375 to 0.02734375
- alpha_row: int32 [324, 1024], replicated, may hold values from 0 to 1023
- alpha_sign: int32 [324, 1024], replicated, may hold values from -1 to 1
- beta_block: int32 [32, 324], P('beta'), may hold values from 0 to 31
- beta_sign: int32 [32, 20736], P('beta'), may hold values from -1 to 1
- block_irrep: int32 [16], replicated, may hold values from 0 to 7, as said below
Outputs:
- sigma: float32 [1024, 2048], P('alpha', 'beta')
Inputs may be any that keep to these rules, and one draw needn't show every extreme that they name: `block_irrep`: irrep 0 is the window's. The 4 blocks held by one index of alpha include 1 to 4 blocks of irrep 0, and some index holds 4 of them.
All inputs are finite; a program needn't handle non-finite values.
Results may differ from a plain program's by a relative error of at most 0.0003.
Values may be sent and summed in bfloat16 or wider, within the bound.
No kernel may reach another device: no remote copies, remote signals or barrier semaphores. Data moves between devices by JAX's collectives and lax.ppermute only.
A program may use at most 128 MiB of HBM per device.

v0:
```python
import jax
import jax.numpy as jnp
from jax import lax
from jax.sharding import PartitionSpec as P


def locate(target_rank, live_flags, per_device):
    block_iota = jnp.arange(live_flags.shape[0], dtype=jnp.int32)
    ranks_all = jnp.cumsum(live_flags) - live_flags
    matches = (live_flags == 1) & (ranks_all == target_rank)
    block_id = jnp.sum(jnp.where(matches, block_iota, 0))
    owner_id = block_id // per_device
    before = jnp.sum(jnp.where(block_iota < owner_id * per_device, live_flags, 0))
    return (block_id, owner_id, target_rank - before)


def block_terms(
    block_id,
    coeff_blocks,
    alpha_row,
    alpha_sign,
    integrals,
    target_table,
    beta_signs,
    block_len,
    total_blocks,
):
    src_blocks = coeff_blocks.shape[0]
    pair_count = integrals.shape[0]
    step_rows = min(16, block_len)
    pieces = []
    for sub_step in range(block_len // step_rows):
        first_row = block_id * block_len + sub_step * step_rows
        row_ids = lax.dynamic_slice_in_dim(alpha_row, first_row, step_rows, 1)
        sign_vals = lax.dynamic_slice_in_dim(alpha_sign, first_row, step_rows, 1).astype(
            jnp.bfloat16
        )
        picked = coeff_blocks[:, row_ids, :] * sign_vals[None, :, :, None]
        picked = picked.reshape(src_blocks, pair_count, step_rows * block_len)
        mixed_rows = jnp.einsum(
            "qp,spx->sqx", integrals, picked, preferred_element_type=jnp.float32
        )
        weighted = (
            mixed_rows.reshape(src_blocks, pair_count, step_rows, block_len)
            * beta_signs[:, :, None, :]
        )
        summed = jnp.dot(
            target_table,
            weighted.reshape(src_blocks * pair_count, step_rows * block_len),
            precision=lax.Precision.HIGHEST,
            preferred_element_type=jnp.float32,
        )
        pieces.append(
            summed.reshape(total_blocks, step_rows, block_len)
            .transpose(1, 0, 2)
            .reshape(step_rows, total_blocks * block_len)
        )
    return jnp.concatenate(pieces, axis=0)


def on_device(
    coefficients, diagonal, integrals, alpha_row, alpha_sign, beta_block, beta_sign, block_irrep
):
    alpha_rank = lax.axis_index("alpha")
    pair_count = integrals.shape[0]
    local_rows, local_cols = coefficients.shape
    block_len = beta_sign.shape[1] // pair_count
    per_device = local_rows // block_len
    src_blocks = local_cols // block_len
    total_blocks = lax.axis_size("beta") * src_blocks
    gathered = lax.all_gather(coefficients, "alpha", axis=0, tiled=True)
    live_flags = (block_irrep == 0).astype(jnp.int32)
    live_rows = jnp.repeat(live_flags, block_len)
    gathered = gathered * live_rows[:, None].astype(jnp.bfloat16)
    window_rows = gathered.shape[0]
    coeff_blocks = gathered.reshape(window_rows, src_blocks, block_len).transpose(1, 0, 2)
    beta_ids = beta_block.reshape(-1)
    target_iota = jnp.arange(total_blocks, dtype=jnp.int32)
    target_table = (target_iota[:, None] == beta_ids[None, :]).astype(jnp.float32)
    beta_signs = beta_sign.reshape(src_blocks, pair_count, block_len).astype(jnp.float32)
    block_iota = jnp.arange(live_flags.shape[0], dtype=jnp.int32)
    base_own = jnp.sum(jnp.where(block_iota < alpha_rank * per_device, live_flags, 0))
    own_flags = lax.dynamic_slice_in_dim(live_flags, alpha_rank * per_device, per_device, 0)
    own_count = jnp.sum(own_flags)

    def rank_of(slot_idx):
        return base_own + slot_idx

    empty = jnp.zeros((per_device, block_len, total_blocks * block_len), jnp.float32)

    def one_task(slot_idx, buffer):
        block_id, owner_id, live_pos = locate(rank_of(slot_idx), live_flags, per_device)
        rows_out = block_terms(
            block_id,
            coeff_blocks,
            alpha_row,
            alpha_sign,
            integrals,
            target_table,
            beta_signs,
            block_len,
            total_blocks,
        )
        return lax.dynamic_update_index_in_dim(buffer, rows_out, slot_idx, 0)

    buffer = lax.fori_loop(0, own_count, one_task, empty)
    whole = lax.psum(buffer, "beta")
    summed = lax.dynamic_slice_in_dim(whole, lax.axis_index("beta") * local_cols, local_cols, 2)
    own_pos = jnp.cumsum(own_flags) - own_flags
    placed = summed[own_pos]
    placed = jnp.where(own_flags[:, None, None] == 1, placed, jnp.zeros_like(placed)).reshape(
        local_rows, local_cols
    )
    own_live_rows = jnp.repeat(own_flags, block_len)
    total = diagonal * coefficients.astype(jnp.float32) + placed
    return jnp.where(own_live_rows[:, None] == 1, total, jnp.zeros_like(total))


def solution(mesh):
    return jax.shard_map(
        on_device,
        mesh=mesh,
        in_specs=(
            P("alpha", "beta"),
            P("alpha", "beta"),
            P(),
            P(),
            P(),
            P("beta", None),
            P("beta", None),
            P(),
        ),
        out_specs=P("alpha", "beta"),
        check_vma=False,
    )
```

profile of v0, /device:TPU:0, one launch (start us, length us, event | category | flops | bytes accessed | tf_op | source)
XLA Modules:
  0.0 994.1 jit_solution(5264304404803177056)
XLA Ops:
  12.0 15.0 %all_gather.3 = bf16[1024,256]{0,1:T(8,128)(2,1)S(1)} all-gather(bf16[256,256]{0,1:T(8,128)(2,1)S(1)} %copy.31), channel_id=1, replica_groups=mesh['alpha'=4,'beta'=8] {'alpha'}, dimensions={0}, use_global_device_ids=true | all-gather | bytes 655360 | tf_op jit(solution)/shard_map/all_gather | solution.py:71
  32.9 443.5 %while.13 = (s32[]{:T(128)}, f32[4,64,2048]{2,1,0:T(8,128)}, s32[]{:T(128)}, s32[16]{0:T(128)S(1)}, s32[]{:T(128)}, /*index=5*/s32[16]{0:T(128)S(1)}, s32[324,10...) while((s32[]{:T(128)}, f32[4,64,2048]{2,1,0:T(8,128)}, ...), condition=%wide.region_5.6_spmd.clone, body=%wide.region_3.5_spmd.clone.sunk | while | flops 5489734656 | bytes 250860528 | solution.py:106
  37.3 15.2 %gather_fusion.1 = bf16[5184,4,64]{2,1,0:T(4,128)(2,1)} fusion(bf16[4,1024,64]{2,0,1:T(4,128)(2,1)S(1)} %get-tuple-element.379, s32[6144]{0:T(1024)S(1)} %pad_clamp_fusion.10), kind=kCustom, calls=%fused_computation.2.clone.clone.1 | custom fusion | bytes 5329152 | tf_op jit(solution)/shard_map/while/body/gather | solution.py:38
  52.5 10.7 %copy.54 = bf16[324,16,4,64]{0,3,1,2:T(8,128)(2,1)} copy(bf16[324,16,4,64]{3,2,1,0:T(4,128)(2,1)} %bitcast.145) | data formatting | bytes 5308416 | tf_op jit(solution)/shard_map/while/body/gather | solution.py:38
  70.3 4.4 reshape.331
  74.7 6.1 copy.55
  84.7 8.0 mul.225
  92.7 8.4 fusion.86
  101.5 15.2 %gather_fusion.2 = bf16[5184,4,64]{2,1,0:T(4,128)(2,1)} fusion(bf16[4,1024,64]{2,0,1:T(4,128)(2,1)S(1)} %get-tuple-element.379, s32[6144]{0:T(1024)S(1)} %pad_clamp_fusion.11), kind=kCustom, calls=%fused_computation.1.clone.clone.1 | custom fusion | bytes 5329152 | tf_op jit(solution)/shard_map/while/body/gather | solution.py:38
  116.8 10.7 %copy.57 = bf16[324,16,4,64]{0,3,1,2:T(8,128)(2,1)} copy(bf16[324,16,4,64]{3,2,1,0:T(4,128)(2,1)} %bitcast.146) | data formatting | bytes 5308416 | tf_op jit(solution)/shard_map/while/body/gather | solution.py:38
  129.8 4.0 convolution_bitcast_fusion.10
  133.7 4.3 reshape.335
  138.0 6.1 copy.58
  144.2 8.4 fusion.87
  153.0 15.2 %gather_fusion = bf16[5184,4,64]{2,1,0:T(4,128)(2,1)} fusion(bf16[4,1024,64]{2,0,1:T(4,128)(2,1)S(1)} %get-tuple-element.379, s32[6144]{0:T(1024)S(1)} %pad_clamp_fusion.9), kind=kCustom, calls=%fused_computation.3.clone.clone.1 | custom fusion | bytes 5329152 | tf_op jit(solution)/shard_map/while/body/gather | solution.py:38
  168.3 10.7 %copy.51 = bf16[324,16,4,64]{0,3,1,2:T(8,128)(2,1)} copy(bf16[324,16,4,64]{3,2,1,0:T(4,128)(2,1)} %bitcast.147) | data formatting | bytes 5308416 | tf_op jit(solution)/shard_map/while/body/gather | solution.py:38
  185.2 4.3 reshape.327
  189.5 6.1 copy.52
  195.7 8.4 fusion.85
  204.5 15.2 %gather_fusion.3 = bf16[5184,4,64]{2,1,0:T(4,128)(2,1)} fusion(bf16[4,1024,64]{2,0,1:T(4,128)(2,1)S(1)} %get-tuple-element.379, s32[6144]{0:T(1024)S(1)} %pad_clamp_fusion.12), kind=kCustom, calls=%fused_computation.clone.clone.1 | custom fusion | bytes 5329152 | tf_op jit(solution)/shard_map/while/body/gather | solution.py:38
  219.7 10.7 %copy.60 = bf16[324,16,4,64]{0,3,1,2:T(8,128)(2,1)} copy(bf16[324,16,4,64]{3,2,1,0:T(4,128)(2,1)} %bitcast.148) | data formatting | bytes 5308416 | tf_op jit(solution)/shard_map/while/body/gather | solution.py:38
  232.7 4.0 convolution_bitcast_fusion.11
  236.7 4.3 reshape.339
  241.0 6.1 copy.61
  247.1 6.2 fusion.88
  258.7 15.2 %gather_fusion.1 = bf16[5184,4,64]{2,1,0:T(4,128)(2,1)} fusion(bf16[4,1024,64]{2,0,1:T(4,128)(2,1)S(1)} %get-tuple-element.379, s32[6144]{0:T(1024)S(1)} %pad_clamp_fusion.10), kind=kCustom, calls=%fused_computation.2.clone.clone.1 | custom fusion | bytes 5329152 | tf_op jit(solution)/shard_map/while/body/gather | solution.py:38
  274.0 10.7 %copy.54 = bf16[324,16,4,64]{0,3,1,2:T(8,128)(2,1)} copy(bf16[324,16,4,64]{3,2,1,0:T(4,128)(2,1)} %bitcast.145) | data formatting | bytes 5308416 | tf_op jit(solution)/shard_map/while/body/gather | solution.py:38
  291.8 4.4 reshape.331
  296.2 6.1 copy.55
  306.2 8.0 mul.225
  314.2 8.4 fusion.86
  323.0 15.2 %gather_fusion.2 = bf16[5184,4,64]{2,1,0:T(4,128)(2,1)} fusion(bf16[4,1024,64]{2,0,1:T(4,128)(2,1)S(1)} %get-tuple-element.379, s32[6144]{0:T(1024)S(1)} %pad_clamp_fusion.11), kind=kCustom, calls=%fused_computation.1.clone.clone.1 | custom fusion | bytes 5329152 | tf_op jit(solution)/shard_map/while/body/gather | solution.py:38
  338.2 10.7 %copy.57 = bf16[324,16,4,64]{0,3,1,2:T(8,128)(2,1)} copy(bf16[324,16,4,64]{3,2,1,0:T(4,128)(2,1)} %bitcast.146) | data formatting | bytes 5308416 | tf_op jit(solution)/shard_map/while/body/gather | solution.py:38
  351.2 4.0 convolution_bitcast_fusion.10
  355.2 4.3 reshape.335
  359.5 6.1 copy.58
  365.6 8.4 fusion.87
  374.5 15.2 %gather_fusion = bf16[5184,4,64]{2,1,0:T(4,128)(2,1)} fusion(bf16[4,1024,64]{2,0,1:T(4,128)(2,1)S(1)} %get-tuple-element.379, s32[6144]{0:T(1024)S(1)} %pad_clamp_fusion.9), kind=kCustom, calls=%fused_computation.3.clone.clone.1 | custom fusion | bytes 5329152 | tf_op jit(solution)/shard_map/while/body/gather | solution.py:38
  389.7 10.7 %copy.51 = bf16[324,16,4,64]{0,3,1,2:T(8,128)(2,1)} copy(bf16[324,16,4,64]{3,2,1,0:T(4,128)(2,1)} %bitcast.147) | data formatting | bytes 5308416 | tf_op jit(solution)/shard_map/while/body/gather | solution.py:38
  406.7 4.3 reshape.327
  411.0 6.1 copy.52
  417.1 8.4 fusion.85
  426.0 15.2 %gather_fusion.3 = bf16[5184,4,64]{2,1,0:T(4,128)(2,1)} fusion(bf16[4,1024,64]{2,0,1:T(4,128)(2,1)S(1)} %get-tuple-element.379, s32[6144]{0:T(1024)S(1)} %pad_clamp_fusion.12), kind=kCustom, calls=%fused_computation.clone.clone.1 | custom fusion | bytes 5329152 | tf_op jit(solution)/shard_map/while/body/gather | solution.py:38
  441.2 10.7 %copy.60 = bf16[324,16,4,64]{0,3,1,2:T(8,128)(2,1)} copy(bf16[324,16,4,64]{3,2,1,0:T(4,128)(2,1)} %bitcast.148) | data formatting | bytes 5308416 | tf_op jit(solution)/shard_map/while/body/gather | solution.py:38
  458.2 4.3 reshape.339
  462.5 6.1 copy.61
  468.6 6.2 fusion.88
  476.7 508.2 %all-reduce.2.cloned.1.call-done = f32[4,64,2048]{2,1,0:T(8,128)} async-done(((f32[4,64,2048]{2,1,0:T(8,128)}), f32[4,64,2048]{2,1,0:T(8,128)}) %all-reduce.2.cloned.1.call-update) | async-done | bytes 2097168 | tf_op jit(solution)/shard_map/psum | solution.py:107
  (112 shorter events, 71.0 us)
Async XLA Ops:
  6.5 24.1 %copy-start.2 = (s32[4,20736]{1,0:T(4,128)S(1)}, s32[4,20736]{1,0:T(4,128)}, u32[]{:S(2)}) copy-start(s32[4,20736]{1,0:T(4,128)} %param.16) | copy-start | bytes 995332
  6.5 24.7 %copy-start.4 = (s32[4,324]{1,0:T(4,128)S(1)}, s32[4,324]{1,0:T(4,128)}, u32[]{:S(2)}) copy-start(s32[4,324]{1,0:T(4,128)} %param.15) | copy-start | bytes 15556
  6.5 978.3 %all-reduce.2.cloned.1.call-start = ((), (), s32[]{:S(2)}) async-start(), calls=%async_computation | async-start | bytes 4194304 | tf_op jit(solution)/shard_map/psum | solution.py:107
  26.9 6.0 copy-start
  32.9 443.6 %copy-start.6 = (pred[4]{0:T(512)(128)(4,1)S(1)}, pred[4]{0:T(512)(128)(4,1)}, u32[]{:S(2)}) copy-start(pred[4]{0:T(512)(128)(4,1)} %get-tuple-element.219) | copy-start | bytes 16
  32.9 443.8 %copy-start.5 = (s32[4]{0:T(128)S(1)}, s32[4]{0:T(128)}, u32[]{:S(2)}) copy-start(s32[4]{0:T(128)} %get-tuple-element.229) | copy-start | bytes 52
  32.9 953.5 %copy-start.1 = (bf16[256,256]{1,0:T(8,128)(2,1)S(1)}, bf16[256,256]{1,0:T(8,128)(2,1)}, u32[]{:S(2)}) copy-start(bf16[256,256]{1,0:T(8,128)(2,1)} %param.10) | copy-start | bytes 393220
  32.9 953.5 %copy-start.3 = (f32[256,256]{1,0:T(8,128)S(1)}, f32[256,256]{1,0:T(8,128)}, u32[]{:S(2)}) copy-start(f32[256,256]{1,0:T(8,128)} %param.11) | copy-start | bytes 786436
Sparse Core Ops, SparseCore 0:
  476.6 508.2 all-reduce.1
where the time goes:
time: 1000 us; the launch traced here: 994 us
  waiting for transfers between devices  508 us (51%)
  local copies, waits for them, and re-layouts  327 us (33%)
  matrix products  94.5 us (9%)
  other arithmetic  30.7 us (3%)
  blocking collectives  15 us (2%)
  between operations  13.5 us (1%)
    psum x1, waiting for transfers between devices, on_device(): whole = lax.psum(buffer, 'beta')  508 us
    gather x16, local copies, waits for them, and re-layouts, block_terms(): picked = coeff_blocks[:, row_ids, :] * sign_vals[None, :, :, None]  207 us
    reshape x14, local copies, waits for them, and re-layouts, block_terms(): mixed_rows.reshape(src_blocks, pair_count, step_rows, block_len)  71.4 us
    dot_general x8, matrix products, block_terms(): jnp.dot(target_table, weighted.reshape(src_blocks * pair_count, step_rows...  62.7 us
    mul x6, local copies, waits for them, and re-layouts, block_terms(): mixed_rows.reshape(src_blocks, pair_count, step_rows, block_len)  35.9 us
    dot_general x8, matrix products, block_terms(): jnp.einsum('qp,spx->sqx', integrals, picked, preferred_element_type=jnp.f...  31.8 us
  transfers between devices with their start and end apart: 1, of which 1 were waited for; matrix products, arithmetic and copies ran while one was open for 0% of the time, Pallas kernels for 0%

commit v1 on v0

v1 whole, which is shorter than its diff:
```python
import functools

import jax
import jax.numpy as jnp
from jax import lax
from jax.experimental import pallas as pl
from jax.experimental.pallas import tpu as pltpu
from jax.sharding import PartitionSpec as P

LANES = 128
VMEM = pl.BlockSpec(memory_space=pltpu.VMEM)
SMEM = pl.BlockSpec(memory_space=pltpu.SMEM)


def round_up(size, step):
    return -(-size // step) * step


class Sizes:
    def __init__(self, coefficients, integrals, alpha_row, beta_sign, block_irrep):
        self.n_alpha = lax.axis_size("alpha")
        self.n_beta = lax.axis_size("beta")
        self.devices = self.n_alpha * self.n_beta
        self.rows, self.cols = coefficients.shape
        self.pairs = integrals.shape[0]
        self.block = beta_sign.shape[1] // self.pairs
        self.src = self.cols // self.block
        self.targets = self.n_beta * self.src
        self.all_rows = alpha_row.shape[1]
        self.blocks = block_irrep.shape[0]
        self.own = self.rows // self.block
        self.share = max(1, self.devices // self.block)
        self.sets = self.devices // self.share
        self.strings = self.block // self.sets
        self.halves = self.rows // LANES
        self.tiles = self.all_rows // LANES
        self.per = max(1, self.src // self.n_alpha)
        self.senders = self.src // self.per
        self.group = self.src * self.strings
        self.lists = self.n_beta * self.group
        self.pair_rows = round_up(self.pairs, 8)
        self.pair_lanes = round_up(self.pairs, LANES)
        self.pair_tiles = self.pair_lanes // LANES
        self.coef_rows = self.halves * self.group
        self.sign_rows = self.per * self.strings * self.pair_tiles
        self.pack = round_up(self.coef_rows + self.sign_rows, 8)


def pack_kernel(z, coef_ref, sign_ref, out_ref, scratch):
    scratch[...] = jnp.zeros_like(scratch)
    turned = coef_ref[...].astype(jnp.float32).T
    for half in range(z.halves):
        for g in range(z.group):
            row = half * z.group + g
            for part in range(z.share):
                scratch[pl.ds(row + part * z.pack, z.sets, stride=z.share * z.pack), :] = turned[
                    g * z.sets : (g + 1) * z.sets, half * LANES : (half + 1) * LANES
                ]
    for s in range(z.per):
        code = sign_ref[s].T
        code = jnp.concatenate(
            [code, jnp.zeros((z.block, z.pair_lanes - z.pairs), jnp.float32)], axis=1
        )
        for cc in range(z.strings):
            for k in range(z.pair_tiles):
                row = z.coef_rows + (s * z.strings + cc) * z.pair_tiles + k
                for part in range(z.share):
                    scratch[pl.ds(row + part * z.pack, z.sets, stride=z.share * z.pack), :] = code[
                        cc * z.sets : (cc + 1) * z.sets, k * LANES : (k + 1) * LANES
                    ]
    out_ref[...] = scratch[...].astype(jnp.bfloat16)


def main_kernel(
    z,
    irrep_ref,
    part_ref,
    rx_ref,
    integ_ref,
    row_ref,
    sign_ref,
    out_ref,
    rxf,
    full,
    table,
    codes,
    weights,
    lane_of,
    chunk_of,
    sign_of,
    acc,
    result,
    rank_ref,
    list_ref,
):
    f32 = jnp.float32
    half_block = z.block
    count = jnp.int32(0)
    lane_row = lax.broadcasted_iota(jnp.int32, (1, LANES), 1)
    ranks = jnp.full((1, LANES), -1, jnp.int32)
    for g in range(z.blocks):
        live = irrep_ref[g] == 0
        rank = jnp.where(live, count, -1)
        rank_ref[g] = rank
        list_ref[count] = g
        ranks = jnp.where(lane_row == g, rank, ranks)
        count = count + live.astype(jnp.int32)
    list_ref[count] = 0
    n_tiles = (count + 1) // 2

    rxf[...] = rx_ref[...].astype(f32)
    for i in range(z.n_alpha):
        base = i * z.n_beta * z.pack
        for half in range(z.halves):
            for g in range(z.group):
                full[i * z.halves + half, pl.ds(g, z.n_beta, stride=z.group), :] = rxf[
                    pl.ds(base + half * z.group + g, z.n_beta, stride=z.pack), :
                ]
        for s in range(z.per if i < z.senders else 0):
            for cc in range(z.strings):
                for k in range(z.pair_tiles):
                    source = base + z.coef_rows + (s * z.strings + cc) * z.pair_tiles + k
                    dest = (i * z.per + s) * z.strings + cc
                    codes[k, pl.ds(dest, z.n_beta, stride=z.group), :] = rxf[
                        pl.ds(source, z.n_beta, stride=z.pack), :
                    ]

    step = min(8, z.lists)
    target = (lax.broadcasted_iota(jnp.int32, (z.targets, z.pair_lanes), 0) + 1).astype(f32)

    def weight_step(n, carry):
        parts = []
        for m in range(step):
            code = jnp.concatenate(
                [codes[k, pl.ds(n * step + m, 1), :] for k in range(z.pair_tiles)], axis=1
            )
            hit = jnp.where(code == target, 1.0, 0.0) - jnp.where(code == -target, 1.0, 0.0)
            parts.append(hit)
        hits = jnp.concatenate(parts, axis=0).astype(jnp.bfloat16)
        found = jnp.dot(hits, integ_ref[...], preferred_element_type=f32)
        high = found.astype(jnp.bfloat16)
        low = (found - high.astype(f32)).astype(jnp.bfloat16)
        for m in range(step):
            rows = slice(m * z.targets, (m + 1) * z.targets)
            weights[n * step + m, 0 : z.targets, :] = high[rows]
            weights[n * step + m, z.targets : 2 * z.targets, :] = low[rows]
        return carry

    lax.fori_loop(0, z.lists // step, weight_step, 0)

    lane_list = lax.broadcasted_iota(jnp.int32, (z.lists, LANES), 1)
    lane_pair = lax.broadcasted_iota(jnp.int32, (z.pairs, LANES), 1)
    tail = z.pair_rows - 8

    def compact_step(u, carry):
        first, second = list_ref[2 * u], list_ref[2 * u + 1]
        left_shift = (first % 2) * half_block
        right_shift = (1 - second % 2) * half_block
        left = pltpu.roll(full[first // 2], left_shift, 1)
        right = pltpu.roll(full[second // 2], right_shift, 1)
        table[u] = jnp.where(lane_list < half_block, left, right)

        def merged(ref):
            at_first = pl.ds(pl.multiple_of(first // 2 * LANES, LANES), LANES)
            at_second = pl.ds(pl.multiple_of(second // 2 * LANES, LANES), LANES)
            return jnp.where(
                lane_pair < half_block,
                pltpu.roll(ref[:, at_first], left_shift, 1),
                pltpu.roll(ref[:, at_second], right_shift, 1),
            )

        source = merged(row_ref)
        signs = merged(sign_ref)
        block = lax.shift_right_logical(source, 6)
        rank = jnp.take_along_axis(
            jnp.broadcast_to(ranks, (z.pairs, LANES)), block, axis=1, mode="promise_in_bounds"
        )
        spot = rank * half_block + (source & (half_block - 1))
        inside = (lane_pair < half_block) | (2 * u + 1 < count)
        used = (rank >= 0) & (signs != 0) & inside
        lane_of[u, tail : z.pair_rows, :] = jnp.zeros((8, LANES), jnp.int32)
        chunk_of[u, tail : z.pair_rows, :] = jnp.full((8, LANES), -1, jnp.int32)
        sign_of[u, tail : z.pair_rows, :] = jnp.zeros((8, LANES), f32)
        lane_of[u, 0 : z.pairs, :] = spot & (LANES - 1)
        chunk_of[u, 0 : z.pairs, :] = jnp.where(used, lax.shift_right_logical(spot, 7), -1)
        sign_of[u, 0 : z.pairs, :] = signs.astype(f32)
        return carry

    lax.fori_loop(0, n_tiles, compact_step, 0)

    groups = z.pair_rows // 8
    padding = jnp.zeros((z.pair_lanes - z.pair_rows, LANES), f32)

    def run(depth):
        def one_tile(u, carry):
            acc[...] = jnp.zeros_like(acc)

            def one_source(s, inner):
                base = s * z.strings
                pieces = [[] for _ in range(z.strings)]
                tables = [
                    [
                        jnp.broadcast_to(table[k, pl.ds(base + cc, 1), :], (8, LANES))
                        for k in range(depth)
                    ]
                    for cc in range(z.strings)
                ]
                for m in range(groups):
                    at = slice(m * 8, m * 8 + 8)
                    lanes = lane_of[u, at, :]
                    chunk = chunk_of[u, at, :]
                    sign = sign_of[u, at, :]
                    hits = [chunk == k for k in range(depth)]
                    for cc in range(z.strings):
                        value = jnp.zeros((8, LANES), f32)
                        for k in range(depth):
                            taken = jnp.take_along_axis(
                                tables[cc][k], lanes, axis=1, mode="promise_in_bounds"
                            )
                            value = jnp.where(hits[k], taken, value)
                        pieces[cc].append(value * sign)
                for cc in range(z.strings):
                    picked = jnp.concatenate(pieces[cc] + [padding], axis=0)
                    acc[cc] += jnp.dot(
                        weights[base + cc], picked.astype(jnp.bfloat16), preferred_element_type=f32
                    )
                return inner

            lax.fori_loop(0, z.targets, one_source, 0)
            for cc in range(z.strings):
                total = acc[cc, 0 : z.targets, :] + acc[cc, z.targets : 2 * z.targets, :]
                result[u, pl.ds(cc, z.targets, stride=z.strings), :] = total
            return carry

        if z.share == 1:
            lax.fori_loop(0, n_tiles, one_tile, 0)
        else:
            part = part_ref[0]
            mine = (n_tiles - part + z.share - 1) // z.share
            lax.fori_loop(0, mine, lambda n, carry: one_tile(n * z.share + part, carry), 0)

    depths = sorted({min(d, z.tiles) for d in (4, 5, 6, 8, z.tiles)})
    lower = 0
    for depth in depths:
        pl.when((n_tiles > lower) & (n_tiles <= depth))(functools.partial(run, depth))
        lower = depth

    wide = z.src * z.strings
    lane_out = lax.broadcasted_iota(jnp.int32, (z.targets * z.strings, LANES), 1)
    for w in range(z.tiles):
        sides = []
        for side in range(2):
            rank = rank_ref[2 * w + side]
            spot = jnp.maximum(rank, 0)
            shift = ((spot + side) % 2) * half_block
            moved = pltpu.roll(result[spot // 2], shift, 1)
            here = rank >= 0
            if z.share > 1:
                here = here & ((spot // 2) % z.share == part_ref[0])
            sides.append(jnp.where(here, moved, 0.0))
        both = jnp.where(lane_out < half_block, sides[0], sides[1])
        for j in range(z.n_beta):
            device = w // z.halves * z.n_beta + j
            out_ref[device, w % z.halves] = both[j * wide : (j + 1) * wide]


def finish_kernel(z, irrep_ref, rx_ref, diag_ref, coef_ref, out_ref):
    wide = z.src * z.strings
    stride = z.share * z.halves * wide

    def column(first):
        rows = [
            rx_ref[pl.ds(part * z.halves * wide + first, z.sets, stride=stride), :]
            for part in range(z.share)
        ]
        return functools.reduce(jnp.add, rows)

    columns = []
    for t in range(z.src):
        for cc in range(z.strings):
            firsts = [h * wide + t * z.strings + cc for h in range(z.halves)]
            columns.append(jnp.concatenate([column(first) for first in firsts], axis=1))
    added = jnp.concatenate(columns, axis=0).T
    total = diag_ref[...] * coef_ref[...].astype(jnp.float32) + added
    for b in range(z.own):
        at = slice(b * z.block, (b + 1) * z.block)
        out_ref[at, :] = jnp.where(irrep_ref[b] == 0, total[at], 0.0)


def on_device(
    coefficients, diagonal, integrals, alpha_row, alpha_sign, beta_block, beta_sign, block_irrep
):
    z = Sizes(coefficients, integrals, alpha_row, beta_sign, block_irrep)
    f32, i32, bf16 = jnp.float32, jnp.int32, jnp.bfloat16
    alpha_rank = lax.axis_index("alpha")
    params = pltpu.CompilerParams(vmem_limit_bytes=56 * 1024 * 1024)

    first = jnp.minimum(alpha_rank, z.senders - 1) * z.per
    own_signs = lax.dynamic_slice_in_dim(beta_sign, first, z.per, 0)
    own_blocks = lax.dynamic_slice_in_dim(beta_block, first, z.per, 0)
    code = own_signs.reshape(z.per, z.pairs, z.block) * (own_blocks + 1)[:, :, None]
    packed = pl.pallas_call(
        functools.partial(pack_kernel, z),
        out_shape=jax.ShapeDtypeStruct((z.devices * z.pack, LANES), bf16),
        in_specs=[VMEM, VMEM],
        out_specs=VMEM,
        scratch_shapes=[pltpu.VMEM((z.devices * z.pack, LANES), f32)],
        compiler_params=params,
    )(coefficients, code.astype(f32))
    arrived = lax.all_to_all(
        packed.reshape(z.devices, z.pack, LANES), ("alpha", "beta"), 0, 0, tiled=True
    ).reshape(z.devices * z.pack, LANES)

    pad = z.pair_lanes - z.pairs
    wide = z.src * z.strings
    part = (alpha_rank * z.n_beta + lax.axis_index("beta")) % z.share
    integ = jnp.pad(integrals, ((0, pad), (0, pad)))
    terms = pl.pallas_call(
        functools.partial(main_kernel, z),
        out_shape=jax.ShapeDtypeStruct((z.devices, z.halves, wide, LANES), f32),
        in_specs=[SMEM, SMEM, VMEM, VMEM, VMEM, VMEM],
        out_specs=VMEM,
        scratch_shapes=[
            pltpu.VMEM((z.devices * z.pack, LANES), f32),
            pltpu.VMEM((z.tiles, z.lists, LANES), f32),
            pltpu.VMEM((z.tiles, z.lists, LANES), f32),
            pltpu.VMEM((z.pair_tiles, z.lists, LANES), f32),
            pltpu.VMEM((z.lists, 2 * z.targets, z.pair_lanes), bf16),
            pltpu.VMEM((z.tiles, z.pair_rows, LANES), i32),
            pltpu.VMEM((z.tiles, z.pair_rows, LANES), i32),
            pltpu.VMEM((z.tiles, z.pair_rows, LANES), f32),
            pltpu.VMEM((z.strings, 2 * z.targets, LANES), f32),
            pltpu.VMEM((z.tiles, z.targets * z.strings, LANES), f32),
            pltpu.SMEM((z.blocks,), i32),
            pltpu.SMEM((z.blocks + 2,), i32),
        ],
        compiler_params=params,
    )(block_irrep, part.astype(i32)[None], arrived, integ, alpha_row, alpha_sign)

    back = lax.all_to_all(terms, ("alpha", "beta"), 0, 0, tiled=True).reshape(-1, LANES)
    own_irrep = lax.dynamic_slice_in_dim(block_irrep, alpha_rank * z.own, z.own, 0)
    return pl.pallas_call(
        functools.partial(finish_kernel, z),
        out_shape=jax.ShapeDtypeStruct((z.rows, z.cols), f32),
        in_specs=[SMEM, VMEM, VMEM, VMEM],
        out_specs=VMEM,
        compiler_params=params,
    )(own_irrep, back, diagonal, coefficients)


def solution(mesh):
    return jax.shard_map(
        on_device,
        mesh=mesh,
        in_specs=(
            P("alpha", "beta"),
            P("alpha", "beta"),
            P(),
            P(),
            P(),
            P("beta", None),
            P("beta", None),
            P(),
        ),
        out_specs=P("alpha", "beta"),
        check_vma=False,
    )
```

time: 1000 us -> 179 us (0.18)
  waiting for transfers between devices: 508 us -> 17.7 us
  local copies, waits for them, and re-layouts: 327 us -> 3.31 us
  Pallas kernels: 0 us -> 146 us
  matrix products: 94.5 us -> 0 us
  other arithmetic: 30.7 us -> 1.54 us
  blocking collectives: 15 us -> 0 us
  between operations: 13.5 us -> 0.06 us
    psum x1 -> x0, waiting for transfers between devices: 508 us -> none  [on_device(): whole = lax.psum(buffer, 'beta')]
    gather x17 -> x0, local copies, waits for them, and re-layouts: 208 us -> none  [the longest x16 207 us: block_terms(): picked = coeff_blocks[:, row_ids, :] * sign_vals[None, :, :, None]]
    pallas_call x0 -> x3, Pallas kernels: none -> 146 us  [the longest x1 142 us: on_device(): pl.pallas_call(functools.partial(main_kernel, z), out_shape=jax.ShapeDtyp...]
    dot_general x16 -> x0, matrix products: 94.5 us -> none  [the longest x8 62.7 us: block_terms(): jnp.dot(target_table, weighted.reshape(src_blocks * pair_count, step_rows...]
    reshape x30 -> x1, local copies, waits for them, and re-layouts: 73.2 us -> 0.09 us  [on_device(): own_signs.reshape(z.per, z.pairs, z.block) * (own_blocks + 1)[:, :, None]]
    mul x14 -> x0, local copies, waits for them, and re-layouts: 36.5 us -> none  [the longest x6 35.9 us: block_terms(): mixed_rows.reshape(src_blocks, pair_count, step_rows, block_len)]
    mul x9 -> x0, other arithmetic: 17.9 us -> none  [the longest x8 17.9 us: block_terms(): picked = coeff_blocks[:, row_ids, :] * sign_vals[None, :, :, None]]
    all_to_all x0 -> x2, waiting for transfers between devices: none -> 17.7 us  [the longest x1 9.7 us: on_device(): lax.all_to_all(terms, ('alpha', 'beta'), 0, 0, tiled=True)]
  transfers between devices with their start and end apart: 1 -> 2, of which waited for: 1 -> 2; matrix products, arithmetic and copies ran while one was open for 0% -> 1% of each run, Pallas kernels for 0% -> 0%
where the time goes in v1:
time: 179 us
  Pallas kernels  146 us (82%)
  waiting for transfers between devices  17.7 us (10%)
  starting transfers between devices  10 us (6%)
  local copies, waits for them, and re-layouts  3.31 us (2%)
    pallas_call x1, Pallas kernels, on_device(): pl.pallas_call(functools.partial(main_kernel, z), out_shape=jax.ShapeDtyp...  142 us
    all_to_all x1, waiting for transfers between devices, on_device(): lax.all_to_all(terms, ('alpha', 'beta'), 0, 0, tiled=True)  9.7 us
    all_to_all x1, waiting for transfers between devices, on_device(): lax.all_to_all(packed.reshape(z.devices, z.pack, LANES), ('alpha', 'beta'...  8 us
    all_to_all x1, starting transfers between devices, on_device(): lax.all_to_all(packed.reshape(z.devices, z.pack, LANES), ('alpha', 'beta'...  7.3 us
  transfers between devices with their start and end apart: 2, of which 2 were waited for; matrix products, arithmetic and copies ran while one was open for 1% of the time, Pallas kernels for 0%

profile of v1, /device:TPU:0, one launch (start us, length us, event | category | flops | bytes accessed | tf_op | source)
XLA Modules:
  0.0 178.5 jit_solution(1427578407383235647)
XLA Ops:
  0.0 0.0 copy-start
  0.0 0.0 copy-start.3
  0.0 0.8 add_reduce_fusion
  0.8 0.2 copy-done
  1.0 0.2 dynamic-slice_reduce_fusion
  1.2 0.1 reshape.55
  1.3 0.8 multiply_convert_fusion.sign_ref
  2.1 1.8 %shard_map.82 = bf16[768,128]{1,0:T(8,128)(2,1)} custom-call(bf16[256,256]{1,0:T(8,128)(2,1)} %coef_ref.3, f32[1,324,64]{2,1,0:T(8,128)} %multiply_convert_fusion.sign_ref), custom_call_target="tpu_custom_call" | custom-call | tf_op jit(solution)/shard_map/pallas_call | solution.py:302
  3.9 7.3 %all-to-all-start = ((bf16[32,24,128]{2,1,0:T(8,128)(2,1)}), bf16[32,24,128]{2,1,0:T(8,128)(2,1)S(1)}, u32[]{:S(2)}, u32[]{:S(2)}) async-start(bf16[32,24,128]{2,1,0:T(8,128)(2,1)} %bitcast.5), calls=%async_computation | async-start | bytes 393216 | tf_op jit(solution)/shard_map/all_to_all | solution.py:310
  11.2 0.0 copy-done.3
  11.2 0.7 pad.4.integ_ref
  12.0 8.0 %all-to-all-done = bf16[32,24,128]{2,1,0:T(8,128)(2,1)S(1)} async-done(((bf16[32,24,128]{2,1,0:T(8,128)(2,1)}), bf16[32,24,128]{2,1,0:T(8,128)(2,1)S(1)}, u32[]{:S(2)}, u32[]{:S(2)}) %all-to-all-start) | async-done | bytes 196640 | tf_op jit(solution)/shard_map/all_to_all | solution.py:310
  20.0 0.0 copy-start.2
  20.0 0.7 copy-done.2
  20.6 0.0 copy-start.4
  20.6 142.2 %shard_map.83 = f32[32,2,8,128]{3,2,1,0:T(8,128)} custom-call(s32[16]{0:T(128)} %irrep_ref.1, s32[1]{0:T(128)} %constant.29.clone.1.part_ref, bf16[768,128]{1,0:T(8,128)(2,1)} %bitcast.4, bf16[384,384]{1,0:T(8,128)(2,1)} %pad.4.integ_ref, s32[324,1024]{1,0:T(8,128)} %row_ref.1, s32[324,1024]{1,0:T(8,128)} %sign_ref.1), custom_call_target="tpu_custom_call" | custom-call | tf_op jit(solution)/shard_map/pallas_call | solution.py:318
  162.8 2.7 %all-to-all-start.1 = ((f32[32,2,8,128]{3,2,1,0:T(8,128)}), f32[32,2,8,128]{3,2,1,0:T(8,128)S(1)}, u32[]{:S(2)}, u32[]{:S(2)}) async-start(f32[32,2,8,128]{3,2,1,0:T(8,128)} %shard_map.83), calls=%async_computation.1 | async-start | bytes 524288 | tf_op jit(solution)/shard_map/all_to_all | solution.py:340
  165.5 0.0 copy-done.4
  165.5 0.7 dynamic_slice.9.irrep_ref
  166.2 9.7 %all-to-all-done.1 = f32[32,2,8,128]{3,2,1,0:T(8,128)S(1)} async-done(((f32[32,2,8,128]{3,2,1,0:T(8,128)}), f32[32,2,8,128]{3,2,1,0:T(8,128)S(1)}, u32[]{:S(2)}, u32[]{:S(2)}) %all-to-all-start.1) | async-done | bytes 262176 | tf_op jit(solution)/shard_map/all_to_all | solution.py:340
  175.9 0.0 copy-start.1
  175.9 0.7 copy-done.1
  176.6 1.9 %shard_map.84 = f32[256,256]{1,0:T(8,128)} custom-call(s32[4]{0:T(128)} %dynamic_slice.9.irrep_ref, f32[512,128]{1,0:T(8,128)} %bitcast.3, f32[256,256]{1,0:T(8,128)} %diag_ref.1, bf16[256,256]{1,0:T(8,128)(2,1)} %coef_ref.3), custom_call_target="tpu_custom_call" | custom-call | tf_op jit(solution)/shard_map/pallas_call | solution.py:342
Async XLA Ops:
  0.0 1.0 copy-start
  0.0 11.2 %copy-start.3 = (bf16[324,324]{1,0:T(8,128)(2,1)S(1)}, bf16[324,324]{1,0:T(8,128)(2,1)}, u32[]{:S(2)}) copy-start(bf16[324,324]{1,0:T(8,128)(2,1)} %param.10) | copy-start | bytes 629860
  3.9 16.1 %all-to-all-start = ((bf16[32,24,128]{2,1,0:T(8,128)(2,1)}), bf16[32,24,128]{2,1,0:T(8,128)(2,1)S(1)}, u32[]{:S(2)}, u32[]{:S(2)}) async-start(bf16[32,24,128]{2,1,0:T(8,128)(2,1)} %bitcast.5), calls=%async_computation | async-start | bytes 393216 | tf_op jit(solution)/shard_map/all_to_all | solution.py:310
  20.0 0.7 copy-start.2
  20.6 144.9 %copy-start.4 = (s32[16]{0:T(128)S(1)}, s32[16]{0:T(128)}, u32[]{:S(2)}) copy-start(s32[16]{0:T(128)} %irrep_ref.1) | copy-start | bytes 196
  162.8 13.1 %all-to-all-start.1 = ((f32[32,2,8,128]{3,2,1,0:T(8,128)}), f32[32,2,8,128]{3,2,1,0:T(8,128)S(1)}, u32[]{:S(2)}, u32[]{:S(2)}) async-start(f32[32,2,8,128]{3,2,1,0:T(8,128)} %shard_map.83), calls=%async_computation.1 | async-start | bytes 524288 | tf_op jit(solution)/shard_map/all_to_all | solution.py:340
  175.9 0.7 copy-start.1
